TPU v7x, 32 devices: a whole 2x2x4 slice. The times are simulated.
32 devices in a mesh: tm: 16 (over z, x, core), rows: 2 (over y).
Axes of the slice: x: 2, y: 2, z: 4, core: 2. Of those that a mesh axis runs over, the one named last changes fastest.
Arguments:
- video: bfloat16 [32, 4, 64, 384], P('tm', 'rows'), may hold values from -6 to 6
- conv_weight: bfloat16 [3, 3, 3, 384, 384], replicated, may hold values from -0.0625 to 0.0625
- norm_gain: float32 [384], replicated, may hold values from 0.1 to 1.9
- w_query: bfloat16 [384, 384], replicated, may hold values from -0.3125 to 0.3125
- w_key: bfloat16 [384, 384], replicated, may hold values from -0.875 to 0.875
- w_value: bfloat16 [384, 384], replicated, may hold values from -0.875 to 0.875
- w_out: bfloat16 [384, 384], replicated, may hold values from -0.3125 to 0.3125
- cotangent: bfloat16 [32, 4, 64, 384], P('tm', 'rows'), may hold values from -6 to 6
Outputs:
- block_out: bfloat16 [32, 4, 64, 384], P('tm', 'rows')
- video_grad: bfloat16 [32, 4, 64, 384], P('tm', 'rows')
All inputs are finite; a program needn't handle non-finite values.
Results may differ from a plain program's by a relative error of at most 0.014.
Values may be sent and summed in bfloat16 or wider, within the bound.
A program may use at most 64 MiB of HBM per device.

v0:
```python
import jax
import jax.numpy as jnp
from jax import lax
from jax.sharding import PartitionSpec as P


def padded_2(cells, sides, width):
    for axis, dim in sides:
        count = lax.axis_size(axis)
        ends = count - 1
        head = lax.slice_in_dim(cells, 0, width, axis=dim)
        tail = lax.slice_in_dim(cells, cells.shape[dim] - width, cells.shape[dim], axis=dim)
        cells = jnp.concatenate(
            [
                lax.ppermute(tail, axis, [(i, (i + 1) % count) for i in range(ends)]),
                cells,
                lax.ppermute(head, axis, [((i + 1) % count, i) for i in range(ends)]),
            ],
            axis=dim,
        )
    return cells


def from_behind(value, axis, by):
    devices = lax.axis_size(axis)
    pairs = [(i, i + by) for i in range(devices) if 0 <= i + by < devices]
    return lax.ppermute(value, axis, pairs)


def convolve(padded, kernel, pads):
    result = lax.conv_general_dilated(
        padded[None],
        kernel,
        (1, 1, 1),
        pads,
        dimension_numbers=("NDHWC", "DHWIO", "NDHWC"),
        preferred_element_type=jnp.float32,
    )
    return result[0]


def project(source, weight):
    return jnp.dot(source.reshape(-1, source.shape[-1]), weight, preferred_element_type=jnp.float32)


def local(video, conv_weight, norm_gain, w_query, w_key, w_value, w_out, cotangent):
    frames, height, width, chans = video.shape
    scale = 1.0 / jnp.sqrt(jnp.float32(chans))
    rimmed = padded_2(video, (("rows", 1),), 1)
    cached = from_behind(rimmed, "tm", 1)
    extended = jnp.concatenate([cached, rimmed], axis=0)
    conv = convolve(extended, conv_weight, [(0, 0), (0, 0), (1, 1)]).astype(jnp.bfloat16)
    convf = conv.astype(jnp.float32)
    inverse = lax.rsqrt(jnp.mean(convf * convf, axis=-1, keepdims=True) + 1e-06)
    normed = convf * inverse * norm_gain
    act = jax.nn.silu(normed).astype(jnp.bfloat16)
    shape4 = (frames, height, width, chans)
    queries = project(act, w_query).astype(jnp.bfloat16).reshape(shape4)
    keys = project(act, w_key).astype(jnp.bfloat16).reshape(shape4)
    values = project(act, w_value).astype(jnp.bfloat16).reshape(shape4)
    keys_all, values_all = (
        lax.all_gather(keys, "rows", axis=1, tiled=True),
        lax.all_gather(values, "rows", axis=1, tiled=True),
    )
    query_flat = queries.reshape(frames, -1, chans)
    keys_flat = keys_all.reshape(frames, -1, chans)
    values_flat = values_all.reshape(frames, -1, chans)
    scores = (
        jnp.einsum("fqc,fkc->fqk", query_flat, keys_flat, preferred_element_type=jnp.float32)
        * scale
    )
    top = jnp.max(scores, axis=-1, keepdims=True)
    expo = jnp.exp(scores - top)
    total = jnp.sum(expo, axis=-1, keepdims=True)
    probs = expo / total
    logsum = (top + jnp.log(total))[:, :, 0]
    attended = jnp.einsum(
        "fqk,fkc->fqc", probs.astype(jnp.bfloat16), values_flat, preferred_element_type=jnp.float32
    ).astype(jnp.bfloat16)
    projected = project(attended, w_out)
    block_out = (
        (act.astype(jnp.float32).reshape(-1, chans) + projected)
        .astype(jnp.bfloat16)
        .reshape(shape4)
    )
    grad_att = project(cotangent, w_out.T).astype(jnp.bfloat16).reshape(frames, -1, chans)
    delta = jnp.sum(grad_att.astype(jnp.float32) * attended.astype(jnp.float32), axis=-1)
    probs_again = jnp.exp(scores - logsum[:, :, None])
    dprob = jnp.einsum("fqc,fkc->fqk", grad_att, values_flat, preferred_element_type=jnp.float32)
    dscore = (probs_again * (dprob - delta[:, :, None])).astype(jnp.bfloat16)
    grad_q = (
        jnp.einsum("fqk,fkc->fqc", dscore, keys_flat, preferred_element_type=jnp.float32) * scale
    ).astype(jnp.bfloat16)
    query_all, grad_all = (
        lax.all_gather(queries, "rows", axis=1, tiled=True),
        lax.all_gather(grad_att.reshape(shape4), "rows", axis=1, tiled=True),
    )
    logsum_all, delta_all = (
        lax.all_gather(logsum.reshape(frames, height, width), "rows", axis=1, tiled=True),
        lax.all_gather(delta.reshape(frames, height, width), "rows", axis=1, tiled=True),
    )
    query_wide = query_all.reshape(frames, -1, chans)
    grad_wide = grad_all.reshape(frames, -1, chans)
    own_keys = keys.reshape(frames, -1, chans)
    own_values = values.reshape(frames, -1, chans)
    scores_wide = (
        jnp.einsum("fqc,fkc->fqk", query_wide, own_keys, preferred_element_type=jnp.float32) * scale
    )
    probs_wide = jnp.exp(scores_wide - logsum_all.reshape(frames, -1)[:, :, None])
    dprob_wide = jnp.einsum(
        "fqc,fkc->fqk", grad_wide, own_values, preferred_element_type=jnp.float32
    )
    dscore_wide = (probs_wide * (dprob_wide - delta_all.reshape(frames, -1)[:, :, None])).astype(
        jnp.bfloat16
    )
    grad_k = (
        jnp.einsum("fqk,fqc->fkc", dscore_wide, query_wide, preferred_element_type=jnp.float32)
        * scale
    ).astype(jnp.bfloat16)
    grad_v = jnp.einsum(
        "fqk,fqc->fkc",
        probs_wide.astype(jnp.bfloat16),
        grad_wide,
        preferred_element_type=jnp.float32,
    ).astype(jnp.bfloat16)
    grad_act = cotangent.astype(jnp.float32).reshape(-1, chans)
    grad_act = grad_act + project(grad_q, w_query.T)
    grad_act = grad_act + project(grad_k, w_key.T)
    grad_act = grad_act + project(grad_v, w_value.T)
    grad_act = grad_act.reshape(shape4)
    sigma = jax.nn.sigmoid(normed)
    grad_normed = grad_act * sigma * (1.0 + normed * (1.0 - sigma))
    scaled = grad_normed * norm_gain
    grad_conv = inverse * (
        scaled - convf * inverse * inverse * jnp.mean(scaled * convf, axis=-1, keepdims=True)
    )
    grad_conv = grad_conv.astype(jnp.bfloat16)
    flipped = jnp.transpose(jnp.flip(conv_weight, (0, 1, 2)), (0, 1, 2, 4, 3))
    grad_padded = convolve(grad_conv, flipped, [(2, 2), (2, 2), (1, 1)])
    returned = from_behind(grad_padded[:2].astype(jnp.bfloat16), "tm", -1).astype(jnp.float32)
    grad_rimmed = grad_padded[2:]
    grad_rimmed = grad_rimmed.at[frames - 2 :].add(returned)
    from_below = from_behind(grad_rimmed[:, 0].astype(jnp.bfloat16), "rows", -1).astype(jnp.float32)
    from_above = from_behind(grad_rimmed[:, height + 1].astype(jnp.bfloat16), "rows", 1).astype(
        jnp.float32
    )
    inner = grad_rimmed[:, 1 : height + 1]
    inner = inner.at[:, height - 1].add(from_below)
    inner = inner.at[:, 0].add(from_above)
    video_grad = inner.astype(jnp.bfloat16)
    return (block_out, video_grad)


def solution(mesh):
    return jax.shard_map(
        local,
        mesh=mesh,
        in_specs=(
            P("tm", "rows", None, None),
            P(),
            P(),
            P(),
            P(),
            P(),
            P(),
            P("tm", "rows", None, None),
        ),
        out_specs=(P("tm", "rows", None, None), P("tm", "rows", None, None)),
        check_vma=False,
    )
```

profile of v0, /device:TPU:1, one launch (start us, length us, event | category | flops | bytes accessed | tf_op | source)
XLA Modules:
  0.0 113.7 jit_solution(12112428926908039563)
XLA Ops:
  0.6 1.0 fusion.59
  1.7 4.0 %collective-permute-start = (bf16[2,1,64,384]{3,2,1,0:T(8,128)(2,1)S(1)}, bf16[2,1,64,384]{3,2,1,0:T(8,128)(2,1)S(1)}, u32[]{:S(2)}, u32[]{:S(2)}) collective-permute-start(bf16[2,1,64,384]{3,2,1,0:T(8,128)(2,1)S(1)} %get-tuple-element.63), channel_id=1, source_target_pairs={{0,1},{2,3},{4,5},{6,7},{8,9},{10,11},{12,13},{14,15},{16,17},{18,... | collective-permute-start | bytes 294920 | tf_op jit(solution)/shard_map/ppermute | solution.py:15
  5.6 1.3 %collective-permute-start.1 = (bf16[2,1,64,384]{3,2,1,0:T(8,128)(2,1)S(1)}, bf16[2,1,64,384]{3,2,1,0:T(8,128)(2,1)S(1)}, u32[]{:S(2)}, u32[]{:S(2)}) collective-permute-start(bf16[2,1,64,384]{3,2,1,0:T(8,128)(2,1)S(1)} %get-tuple-element.62), channel_id=1, source_target_pairs={{1,0},{3,2},{5,4},{7,6},{9,8},{11,10},{13,12},{15,14},{17,16},{19,... | collective-permute-start | bytes 294920 | tf_op jit(solution)/shard_map/ppermute | solution.py:17
  8.2 2.8 %collective-permute-done.1 = bf16[2,1,64,384]{3,2,1,0:T(8,128)(2,1)S(1)} collective-permute-done((bf16[2,1,64,384]{3,2,1,0:T(8,128)(2,1)S(1)}, bf16[2,1,64,384]{3,2,1,0:T(8,128)(2,1)S(1)}, u32[]{:S(2)}, u32[]{:S(2)}) %collective-permute-start.1) | collective-permute-done | bytes 98336 | tf_op jit(solution)/shard_map/ppermute | solution.py:17
  11.0 5.1 %collective-permute-start.2 = (bf16[2,4,64,384]{3,2,1,0:T(8,128)(2,1)S(1)}, bf16[2,4,64,384]{3,2,1,0:T(8,128)(2,1)S(1)}, u32[]{:S(2)}, u32[]{:S(2)}) collective-permute-start(bf16[2,4,64,384]{3,2,1,0:T(8,128)(2,1)S(1)} %constant_dynamic-update-slice_fusion), channel_id=1, source_target_pairs={{0,2},{2,4},{4,6},{6,8},{8,10},{10,12},{12,14},{14,16},{16,18},{18... | collective-permute-start | bytes 1179656 | tf_op jit(solution)/shard_map/ppermute | solution.py:27
  16.2 1.5 %convolution_convert_fusion.1 = bf16[256,384]{1,0:T(8,128)(2,1)S(1)} fusion(bf16[256,384]{1,0:T(8,128)(2,1)} %bitcast.116, bf16[384,384]{1,0:T(8,128)(2,1)} %param.22), kind=kOutput, calls=%fused_computation.12 | convolution fusion | flops 75595776 | bytes 688128 | tf_op jit(solution)/shard_map/dot_general | solution.py:43
  17.7 6.2 %all_gather.22 = bf16[2,4,64,384]{3,2,1,0:T(8,128)(2,1)S(1)} all-gather(bf16[2,2,64,384]{3,2,1,0:T(8,128)(2,1)S(1)} %bitcast.99), channel_id=1, replica_groups=mesh['tm'=16,'rows'=2] {'rows'}, dimensions={1}, use_global_device_ids=true | all-gather | bytes 589824 | tf_op jit(solution)/shard_map/all_gather | solution.py:96
  25.3 3.4 %convert_multiply_fusion.2 = (f32[2,2,8,9,384]{4,2,3,1,0:T(8,128)S(1)}, bf16[2,2,8,9,384]{4,2,3,1,0:T(8,128)(2,1)S(1)}) fusion(bf16[3,3,3,384,384]{4,3,2,1,0:T(8,128)(2,1)S(1)} %copy-done.1, bf16[4,4,1,7,2,384]{5,3,4,1,0,2:T(8,128)(2,1)S(1)} %slice.126, bf16[4,4,1,8,9,384]{5,3,4,1,0,2:T(8,128)(2,1)S(1)} %copy.110, pred[8,9]{0,1:T(8,128)(4,1)S(1)} %copy-done.16), kind=kOutput, calls=%fused_computation.82 | convolution fusion | flops 2296922112 | bytes 9683016 | tf_op jit(solution)/shard_map/conv_general_dilated | solution.py:31
  31.2 7.4 %all_gather.19 = bf16[2,4,64,384]{3,2,1,0:T(8,128)(2,1)S(1)} all-gather(bf16[2,2,64,384]{3,2,1,0:T(8,128)(2,1)S(1)} %bitcast.102), channel_id=1, replica_groups=mesh['tm'=16,'rows'=2] {'rows'}, dimensions={1}, use_global_device_ids=true | all-gather | bytes 589824 | tf_op jit(solution)/shard_map/all_gather | solution.py:63
  39.2 6.8 %all_gather.18 = bf16[2,4,64,384]{3,2,1,0:T(8,128)(2,1)S(1)} all-gather(bf16[2,2,64,384]{3,2,1,0:T(8,128)(2,1)S(1)} %bitcast.104), channel_id=1, replica_groups=mesh['tm'=16,'rows'=2] {'rows'}, dimensions={1}, use_global_device_ids=true | all-gather | bytes 589824 | tf_op jit(solution)/shard_map/all_gather | solution.py:62
  47.1 1.0 multiply_reduce_fusion
  48.1 1.1 fusion.3
  49.3 1.1 copy.121
  50.4 1.2 %convolution_add_fusion.2 = f32[256,384]{1,0:T(8,128)S(1)} fusion(bf16[256,384]{1,0:T(8,128)(2,1)} %bitcast.118, bf16[384,384]{1,0:T(8,128)(2,1)S(1)} %copy-done.4, bf16[256,384]{1,0:T(8,128)(2,1)S(1)} %bitcast.117), kind=kOutput, calls=%fused_computation.6 | convolution fusion | flops 75694080 | bytes 1081344 | tf_op jit(solution)/shard_map/dot_general | solution.py:43
  51.7 5.8 %all_gather.20 = bf16[2,4,64,384]{3,2,1,0:T(8,128)(2,1)S(1)} all-gather(bf16[2,2,64,384]{3,2,1,0:T(8,128)(2,1)S(1)} %bitcast.107), channel_id=1, replica_groups=mesh['tm'=16,'rows'=2] {'rows'}, dimensions={1}, use_global_device_ids=true | all-gather | bytes 589824 | tf_op jit(solution)/shard_map/all_gather | solution.py:95
  58.2 3.2 %all_gather.21 = f32[2,4,64]{2,0,1:T(2,128)S(1)} all-gather(f32[2,2,64]{2,0,1:T(2,128)S(1)} %copy.115), channel_id=1, replica_groups=mesh['tm'=16,'rows'=2] {'rows'}, dimensions={1}, use_global_device_ids=true | all-gather | bytes 3072 | tf_op jit(solution)/shard_map/all_gather | solution.py:99
  61.4 3.4 %all_gather.23 = f32[2,4,64]{2,0,1:T(2,128)S(1)} all-gather(f32[2,2,64]{2,0,1:T(2,128)S(1)} %copy.117), channel_id=1, replica_groups=mesh['tm'=16,'rows'=2] {'rows'}, dimensions={1}, use_global_device_ids=true | all-gather | bytes 3072 | tf_op jit(solution)/shard_map/all_gather | solution.py:100
  67.7 17.7 %convolution_select_fusion = f32[4,4,8,9,384]{4,2,3,1,0:T(8,128)S(1)} fusion(bf16[3,3,3,384,384]{4,3,2,1,0:T(8,128)(2,1)} %param.17, pred[8,9]{0,1:T(8,128)(4,1)S(1)} %copy-done.17, bf16[2,2,1,7,2,384]{5,3,4,1,0,2:T(8,128)(2,1)S(1)} %slice.130, bf16[2,2,1,8,9,384]{5,3,4,1,0,2:T(8,128)(2,1)S(1)} %copy.125), kind=kOutput, calls=%fused_computation.2 | convolution fusion | flops 2294489088 | bytes 9996360 | tf_op jit(solution)/shard_map/conv_general_dilated | solution.py:31
  85.8 6.4 %collective-permute-start.3 = (bf16[2,4,64,384]{3,1,2,0:T(4,128)(2,1)S(1)}, bf16[2,4,64,384]{3,1,2,0:T(4,128)(2,1)S(1)}, u32[]{:S(2)}, u32[]{:S(2)}) collective-permute-start(bf16[2,4,64,384]{3,1,2,0:T(4,128)(2,1)S(1)} %slice_bitcast_fusion.1), channel_id=1, source_target_pairs={{2,0},{4,2},{6,4},{8,6},{10,8},{12,10},{14,12},{16,14},{18,16},{20... | collective-permute-start | bytes 1179656 | tf_op jit(solution)/shard_map/ppermute | solution.py:27
  92.5 6.2 %collective-permute-done.3 = bf16[2,4,64,384]{3,1,2,0:T(4,128)(2,1)S(1)} collective-permute-done((bf16[2,4,64,384]{3,1,2,0:T(4,128)(2,1)S(1)}, bf16[2,4,64,384]{3,1,2,0:T(4,128)(2,1)S(1)}, u32[]{:S(2)}, u32[]{:S(2)}) %collective-permute-start.3) | collective-permute-done | bytes 393248 | tf_op jit(solution)/shard_map/ppermute | solution.py:27
  99.3 1.3 %collective-permute-start.4 = (bf16[2,64,384]{2,1,0:T(8,128)(2,1)S(1)}, bf16[2,64,384]{2,1,0:T(8,128)(2,1)S(1)}, u32[]{:S(2)}, u32[]{:S(2)}) collective-permute-start(bf16[2,64,384]{2,1,0:T(8,128)(2,1)S(1)} %bitcast.123), channel_id=1, source_target_pairs={{1,0},{3,2},{5,4},{7,6},{9,8},{11,10},{13,12},{15,14},{17,16},{19,... | collective-permute-start | bytes 294920 | tf_op jit(solution)/shard_map/ppermute | solution.py:27
  101.8 4.0 %collective-permute-start.5 = (bf16[2,64,384]{2,1,0:T(8,128)(2,1)S(1)}, bf16[2,64,384]{2,1,0:T(8,128)(2,1)S(1)}, u32[]{:S(2)}, u32[]{:S(2)}) collective-permute-start(bf16[2,64,384]{2,1,0:T(8,128)(2,1)S(1)} %bitcast.124), channel_id=1, source_target_pairs={{0,1},{2,3},{4,5},{6,7},{8,9},{10,11},{12,13},{14,15},{16,17},{18,... | collective-permute-start | bytes 294920 | tf_op jit(solution)/shard_map/ppermute | solution.py:27
  106.1 3.2 %scatter-add.6 = f32[2,2,64,384]{3,1,2,0:T(2,128)S(1)} dynamic-update-slice(f32[2,2,64,384]{3,1,2,0:T(2,128)S(1)} %slice.135, f32[2,1,64,384]{3,1,2,0:T(1,128)S(1)} %slice_add_fusion.1, s32[]{:T(128)} %constant.106.clone.1, s32[]{:T(128)} %constant.107.clone.1, s32[]{:T(128)} %constant.106.clone.1, s32[]{:T(128)} %constant.106.clone.1) | dynamic-update-slice | bytes 393220 | tf_op jit(solution)/shard_map/scatter-add | solution.py:148
  109.6 3.2 %scatter-add.9 = f32[2,2,64,384]{3,1,2,0:T(2,128)S(1)} dynamic-update-slice(f32[2,2,64,384]{3,1,2,0:T(2,128)S(1)} %scatter-add.6, f32[2,1,64,384]{3,1,2,0:T(1,128)S(1)} %slice_add_fusion, s32[]{:T(128)} %constant.106.clone.1, s32[]{:T(128)} %constant.106.clone.1, s32[]{:T(128)} %constant.106.clone.1, s32[]{:T(128)} %constant.106.clone.1) | dynamic-update-slice | bytes 393220 | tf_op jit(solution)/shard_map/scatter-add | solution.py:149
  (101 shorter events, 14.3 us)
Async XLA Ops:
  0.6 30.3 %copy-start = (bf16[384,384]{1,0:T(8,128)(2,1)S(1)}, bf16[384,384]{1,0:T(8,128)(2,1)}, u32[]{:S(2)}) copy-start(bf16[384,384]{1,0:T(8,128)(2,1)} %param.21) | copy-start | bytes 884740
  1.7 5.6 %collective-permute-start = (bf16[2,1,64,384]{3,2,1,0:T(8,128)(2,1)S(1)}, bf16[2,1,64,384]{3,2,1,0:T(8,128)(2,1)S(1)}, u32[]{:S(2)}, u32[]{:S(2)}) collective-permute-start(bf16[2,1,64,384]{3,2,1,0:T(8,128)(2,1)S(1)} %get-tuple-element.63), channel_id=1, source_target_pairs={{0,1},{2,3},{4,5},{6,7},{8,9},{10,11},{12,13},{14,15},{16,17},{18,... | collective-permute-start | bytes 294920 | tf_op jit(solution)/shard_map/ppermute | solution.py:15
  5.6 5.4 %collective-permute-start.1 = (bf16[2,1,64,384]{3,2,1,0:T(8,128)(2,1)S(1)}, bf16[2,1,64,384]{3,2,1,0:T(8,128)(2,1)S(1)}, u32[]{:S(2)}, u32[]{:S(2)}) collective-permute-start(bf16[2,1,64,384]{3,2,1,0:T(8,128)(2,1)S(1)} %get-tuple-element.62), channel_id=1, source_target_pairs={{1,0},{3,2},{5,4},{7,6},{9,8},{11,10},{13,12},{15,14},{17,16},{19,... | collective-permute-start | bytes 294920 | tf_op jit(solution)/shard_map/ppermute | solution.py:17
  11.0 12.8 %collective-permute-start.2 = (bf16[2,4,64,384]{3,2,1,0:T(8,128)(2,1)S(1)}, bf16[2,4,64,384]{3,2,1,0:T(8,128)(2,1)S(1)}, u32[]{:S(2)}, u32[]{:S(2)}) collective-permute-start(bf16[2,4,64,384]{3,2,1,0:T(8,128)(2,1)S(1)} %constant_dynamic-update-slice_fusion), channel_id=1, source_target_pairs={{0,2},{2,4},{4,6},{6,8},{8,10},{10,12},{12,14},{14,16},{16,18},{18... | collective-permute-start | bytes 1179656 | tf_op jit(solution)/shard_map/ppermute | solution.py:27
  16.1 9.0 %copy-start.1 = (bf16[3,3,3,384,384]{4,3,2,1,0:T(8,128)(2,1)S(1)}, bf16[3,3,3,384,384]{4,3,2,1,0:T(8,128)(2,1)}, u32[]{:S(2)}) copy-start(bf16[3,3,3,384,384]{4,3,2,1,0:T(8,128)(2,1)} %param.17) | copy-start | bytes 23887876
  24.6 0.7 copy-start.16
  28.6 0.7 copy-start.5
  28.6 2.1 %copy-start.12 = (f32[384]{0:T(512)S(1)}, f32[384]{0:T(512)}, u32[]{:S(2)}) copy-start(f32[384]{0:T(512)} %param.18) | copy-start | bytes 4612
  28.6 10.0 %copy-start.4 = (bf16[384,384]{1,0:T(8,128)(2,1)S(1)}, bf16[384,384]{1,0:T(8,128)(2,1)}, u32[]{:S(2)}) copy-start(bf16[384,384]{1,0:T(8,128)(2,1)} %param.19) | copy-start | bytes 884740
  29.5 9.4 %copy-start.2 = (bf16[384,384]{1,0:T(8,128)(2,1)S(1)}, bf16[384,384]{1,0:T(8,128)(2,1)}, u32[]{:S(2)}) copy-start(bf16[384,384]{1,0:T(8,128)(2,1)} %param.20) | copy-start | bytes 884740
  29.5 1.2 %copy-start.6 = (bf16[2,2,1,64,384]{4,3,2,1,0:T(8,128)(2,1)}, bf16[2,2,1,64,384]{4,3,2,1,0:T(8,128)(2,1)S(1)}, u32[]{:S(2)}) copy-start(bf16[2,2,1,64,384]{4,3,2,1,0:T(8,128)(2,1)S(1)} %copy.133) | copy-start | bytes 589828
  30.1 0.6 copy-start.10
  30.7 7.9 %copy-start.14 = (f32[256]{0:T(256)}, f32[256]{0:T(256)S(1)}, u32[]{:S(2)}) copy-start(f32[256]{0:T(256)S(1)} %rsqrt.13) | copy-start | bytes 3076
  46.3 4.2 %copy-start.8 = (bf16[2,2,64,384]{3,2,1,0:T(8,128)(2,1)S(1)}, bf16[2,2,64,384]{3,2,1,0:T(8,128)(2,1)}, u32[]{:S(2)}) copy-start(bf16[2,2,64,384]{3,2,1,0:T(8,128)(2,1)} %param.23) | copy-start | bytes 589828
  64.9 1.4 %copy-start.7 = (bf16[2,2,1,64,384]{4,3,2,1,0:T(8,128)(2,1)S(1)}, bf16[2,2,1,64,384]{4,3,2,1,0:T(8,128)(2,1)}, u32[]{:S(2)}) copy-start(bf16[2,2,1,64,384]{4,3,2,1,0:T(8,128)(2,1)} %copy-done.6) | copy-start | bytes 589828
  64.9 1.4 %copy-start.13 = (f32[384]{0:T(512)S(1)}, f32[384]{0:T(512)}, u32[]{:S(2)}) copy-start(f32[384]{0:T(512)} %param.18) | copy-start | bytes 4612
  64.9 1.4 %copy-start.15 = (f32[256]{0:T(256)S(1)}, f32[256]{0:T(256)}, u32[]{:S(2)}) copy-start(f32[256]{0:T(256)} %copy-done.14) | copy-start | bytes 3076
  66.3 0.7 copy-start.11
  66.8 1.0 copy-start.17
  85.8 12.9 %collective-permute-start.3 = (bf16[2,4,64,384]{3,1,2,0:T(4,128)(2,1)S(1)}, bf16[2,4,64,384]{3,1,2,0:T(4,128)(2,1)S(1)}, u32[]{:S(2)}, u32[]{:S(2)}) collective-permute-start(bf16[2,4,64,384]{3,1,2,0:T(4,128)(2,1)S(1)} %slice_bitcast_fusion.1), channel_id=1, source_target_pairs={{2,0},{4,2},{6,4},{8,6},{10,8},{12,10},{14,12},{16,14},{18,16},{20... | collective-permute-start | bytes 1179656 | tf_op jit(solution)/shard_map/ppermute | solution.py:27
  92.5 8.1 %copy-start.3 = (bf16[384,384]{1,0:T(8,128)(2,1)S(1)}, bf16[384,384]{1,0:T(8,128)(2,1)}, u32[]{:S(2)}) copy-start(bf16[384,384]{1,0:T(8,128)(2,1)} %param.22) | copy-start | bytes 884740
  92.5 8.1 %copy-start.9 = (bf16[2,128,384]{2,1,0:T(8,128)(2,1)S(1)}, bf16[2,128,384]{2,1,0:T(8,128)(2,1)}, u32[]{:S(2)}) copy-start(bf16[2,128,384]{2,1,0:T(8,128)(2,1)} %get-tuple-element.69) | copy-start | bytes 589828
  99.3 6.5 %collective-permute-start.4 = (bf16[2,64,384]{2,1,0:T(8,128)(2,1)S(1)}, bf16[2,64,384]{2,1,0:T(8,128)(2,1)S(1)}, u32[]{:S(2)}, u32[]{:S(2)}) collective-permute-start(bf16[2,64,384]{2,1,0:T(8,128)(2,1)S(1)} %bitcast.123), channel_id=1, source_target_pairs={{1,0},{3,2},{5,4},{7,6},{9,8},{11,10},{13,12},{15,14},{17,16},{19,... | collective-permute-start | bytes 294920 | tf_op jit(solution)/shard_map/ppermute | solution.py:27
  101.8 7.6 %collective-permute-start.5 = (bf16[2,64,384]{2,1,0:T(8,128)(2,1)S(1)}, bf16[2,64,384]{2,1,0:T(8,128)(2,1)S(1)}, u32[]{:S(2)}, u32[]{:S(2)}) collective-permute-start(bf16[2,64,384]{2,1,0:T(8,128)(2,1)S(1)} %bitcast.124), channel_id=1, source_target_pairs={{0,1},{2,3},{4,5},{6,7},{8,9},{10,11},{12,13},{14,15},{16,17},{18,... | collective-permute-start | bytes 294920 | tf_op jit(solution)/shard_map/ppermute | solution.py:27
where the time goes:
time: 114 us
  blocking collectives  32.7 us (29%)
  matrix products  29.8 us (26%)
  starting transfers between devices  22 us (19%)
  local copies, waits for them, and re-layouts  16.7 us (15%)
  waiting for transfers between devices  9.27 us (8%)
  other arithmetic  1.95 us (2%)
  between operations  1.26 us (1%)
    conv_general_dilated x2, matrix products, convolve(): lax.conv_general_dilated(padded[None], kernel, (1, 1, 1), pads, dimension...  21.1 us
    ppermute x4, starting transfers between devices, from_behind(): return lax.ppermute(value, axis, pairs)  16.8 us
    all_gather x1, blocking collectives, local(): lax.all_gather(values, 'rows', axis=1, tiled=True)  7.38 us
    all_gather x1, blocking collectives, local(): lax.all_gather(keys, 'rows', axis=1, tiled=True)  6.76 us
    all_gather x1, blocking collectives, local(): lax.all_gather(grad_att.reshape(shape4), 'rows', axis=1, tiled=True)  6.2 us
    ppermute x4, waiting for transfers between devices, from_behind(): return lax.ppermute(value, axis, pairs)  6.19 us
    all_gather x1, blocking collectives, local(): lax.all_gather(queries, 'rows', axis=1, tiled=True)  5.84 us
    dot_general x8, matrix products, project(): jnp.dot(source.reshape(-1, source.shape[-1]), weight, preferred_element_t...  5.21 us
  transfers between devices with their start and end apart: 6, of which 3 were waited for; matrix products, arithmetic and copies ran while one was open for 7% of the time, Pallas kernels for 0%

commit v1 on v0

v1 whole, which is shorter than its diff:
```python
import functools

import jax
import jax.numpy as jnp
from jax import lax
from jax.experimental import pallas as pl
from jax.experimental.pallas import tpu as pltpu
from jax.sharding import PartitionSpec as P

TAPS = 3
BF = jnp.bfloat16
F32 = jnp.float32


def mm(a, b):
    return lax.dot_general(a, b, (((1,), (0,)), ((), ())), preferred_element_type=F32)


def mm_nt(a, b):
    return lax.dot_general(a, b, (((1,), (1,)), ((), ())), preferred_element_type=F32)


def mm_tn(a, b):
    return lax.dot_general(a, b, (((0,), (0,)), ((), ())), preferred_element_type=F32)


def block(
    n_tm,
    n_rows,
    video,
    weight,
    gain,
    w_query,
    w_key,
    w_value,
    w_out,
    cot,
    block_out,
    video_grad,
    xin,
    wbuf,
    wqkv,
    wo,
    cot_full,
    conv_full,
    sums,
    act_s,
    att_s,
    gc_full,
    gwin,
    w_sem,
    p_sem,
    io_sem,
    halo_send,
    halo_recv,
    cot_send,
    cot_recv,
    conv_send,
    conv_recv,
    gc_send,
    gc_recv,
):
    frames, h, width, chans = video.shape
    full = n_rows * h
    pos = full * width
    own = frames * h * width
    tm = lax.axis_index("tm")
    row = lax.axis_index("rows")
    scale = 1.0 / jnp.sqrt(jnp.float32(chans))
    first_row, last_row = row == 0, row == n_rows - 1
    has_up, has_down = row > 0, row < n_rows - 1
    has_prev, has_next = tm > 0, tm < n_tm - 1
    own_rows = pl.ds(row * h, h)

    w_copies = {
        (a, b): pltpu.make_async_copy(weight.at[a, b], wbuf.at[a, b], w_sem.at[a, b])
        for a in range(TAPS)
        for b in range(TAPS)
    }
    in_copy = pltpu.make_async_copy(video, xin.at[pl.ds(2, frames), pl.ds(1, h)], io_sem.at[0])
    cot_copy = pltpu.make_async_copy(cot, cot_full.at[:, own_rows], io_sem.at[1])
    p_copies = [
        pltpu.make_async_copy(w, wqkv.at[:, pl.ds(i * chans, chans)], p_sem.at[i])
        for i, w in enumerate((w_query, w_key, w_value))
    ] + [pltpu.make_async_copy(w_out, wo, p_sem.at[3])]

    in_copy.start()
    for a in (2, 1, 0):
        for b in range(TAPS):
            w_copies[a, b].start()
    cot_copy.start()
    for c in p_copies:
        c.start()

    barrier = pltpu.get_barrier_semaphore()

    def greet(cond, t, r):
        @pl.when(cond)
        def _():
            pl.semaphore_signal(
                barrier, inc=1, device_id=(t, r), device_id_type=pl.DeviceIdType.MESH
            )

    peers = [lax.rem(row + k, n_rows) for k in range(1, n_rows)]
    for peer in peers:
        pl.semaphore_signal(
            barrier, inc=1, device_id=(tm, peer), device_id_type=pl.DeviceIdType.MESH
        )
    greet(has_prev, tm - 1, row)
    greet(has_prev & has_up, tm - 1, row - 1)
    greet(has_prev & has_down, tm - 1, row + 1)
    greet(has_next, tm + 1, row)

    line = jnp.zeros((frames, width, chans), BF)

    @pl.when(first_row)
    def _():
        xin[2 : 2 + frames, 0] = line
        xin[0:2, 0] = jnp.zeros((2, width, chans), BF)

    @pl.when(last_row)
    def _():
        xin[2 : 2 + frames, h + 1] = line
        xin[0:2, h + 1] = jnp.zeros((2, width, chans), BF)

    @pl.when(tm == 0)
    def _():
        xin[0:2] = jnp.zeros((2, h + 2, width, chans), BF)

    @pl.when(tm == n_tm - 1)
    def _():
        gwin[frames : frames + 2] = jnp.zeros((2, h + 2, width, chans), BF)

    gc_full[0] = jnp.zeros((width, chans), BF)
    gc_full[full + 1] = jnp.zeros((width, chans), BF)

    wait_for = (
        (n_rows - 1)
        + jnp.where(has_prev, 1, 0)
        + jnp.where(has_next, 1 + jnp.where(has_up, 1, 0) + jnp.where(has_down, 1, 0), 0)
    )
    pl.semaphore_wait(barrier, wait_for)

    def remote(src, dst, send, recv, t, r):
        return pltpu.make_async_remote_copy(
            src_ref=src,
            dst_ref=dst,
            send_sem=send,
            recv_sem=recv,
            device_id=(t, r),
            device_id_type=pl.DeviceIdType.MESH,
        )

    now, before = pl.ds(2, frames), pl.ds(0, 2)
    late = pl.ds(frames - 2, 2)
    top, low = pl.ds(0, 1), pl.ds(h - 1, 1)
    halos = [
        (has_up, remote(video.at[:, top], xin.at[now, pl.ds(h + 1, 1)], halo_send.at[0], halo_recv.at[0], tm, row - 1), has_down),
        (has_down, remote(video.at[:, low], xin.at[now, pl.ds(0, 1)], halo_send.at[1], halo_recv.at[1], tm, row + 1), has_up),
        (has_next & has_up, remote(video.at[late, top], xin.at[before, pl.ds(h + 1, 1)], halo_send.at[2], halo_recv.at[2], tm + 1, row - 1), has_prev & has_down),
        (has_next & has_down, remote(video.at[late, low], xin.at[before, pl.ds(0, 1)], halo_send.at[3], halo_recv.at[3], tm + 1, row + 1), has_prev & has_up),
        (has_next, remote(video.at[late], xin.at[before, pl.ds(1, h)], halo_send.at[4], halo_recv.at[4], tm + 1, row), has_prev),
    ]
    for cond, copy, _ in halos:
        pl.when(cond)(copy.start)

    def conv_step(a):
        lhs = jnp.concatenate(
            [xin[a : a + frames, b : b + h].reshape(own, chans) for b in range(TAPS)], axis=1
        )
        rhs = jnp.concatenate(
            [wbuf[a, :, c].reshape(TAPS * chans, chans) for c in range(TAPS)], axis=1
        )
        return mm(lhs, rhs)

    column = lax.rem(lax.broadcasted_iota(jnp.int32, (own, 1), 0), width)

    def shifted(x, by):
        rolled = pltpu.roll(x, by % own, 0)
        edge = column == (0 if by == 1 else width - 1)
        return jnp.where(edge, 0.0, rolled)

    def part(c):
        return sums[:, c * chans : (c + 1) * chans]

    in_copy.wait()
    for _, copy, cond in halos[:2]:
        pl.when(cond)(copy.wait_recv)
    for b in range(TAPS):
        w_copies[2, b].wait()
    sums[...] = conv_step(2)
    cots = [
        remote(cot, cot_full.at[:, own_rows], cot_send.at[k], cot_recv.at[k], tm, peer)
        for k, peer in enumerate(peers)
    ]
    for copy in cots:
        copy.start()
    for _, copy, cond in halos[2:]:
        pl.when(cond)(copy.wait_recv)
    for a in (1, 0):
        for b in range(TAPS):
            w_copies[a, b].wait()
        sums[...] += conv_step(a)
    conv = (shifted(part(0), 1) + part(1) + shifted(part(2), -1)).astype(BF)
    conv_full[:, own_rows] = conv.reshape(frames, h, width, chans)
    convs = [
        remote(
            conv_full.at[:, own_rows],
            conv_full.at[:, own_rows],
            conv_send.at[k],
            conv_recv.at[k],
            tm,
            peer,
        )
        for k, peer in enumerate(peers)
    ]
    for copy in convs:
        copy.start()
    for c in p_copies:
        c.wait()
    cot_copy.wait()
    for copy in cots:
        copy.wait_recv()
    for copy in convs:
        copy.wait_recv()

    g = gain[...]
    mine = pl.ds(pl.multiple_of(row * (h * width), h * width), h * width)
    backs = []
    for f in range(frames):
        convf = conv_full[f].reshape(pos, chans).astype(F32)
        inverse = lax.rsqrt(jnp.mean(convf * convf, axis=-1, keepdims=True) + 1e-06)
        normed = convf * inverse * g
        sigma = 1.0 / (1.0 + jnp.exp(-normed))
        act = (normed * sigma).astype(BF)
        act_s[...] = act
        qkv = mm(act, wqkv[...]).astype(BF)
        query = qkv[:, :chans]
        key = qkv[:, chans : 2 * chans]
        value = qkv[:, 2 * chans :]
        cot_f = cot_full[f].reshape(pos, chans)
        grad_att = mm_nt(cot_f, wo[...]).astype(BF)
        scores = mm_nt(query, key) * scale
        peak = jnp.max(scores, axis=-1, keepdims=True)
        expo = jnp.exp(scores - peak)
        probs = expo / jnp.sum(expo, axis=-1, keepdims=True)
        probs_b = probs.astype(BF)
        attended = mm(probs_b, value).astype(BF)
        att_s[...] = attended
        delta = jnp.sum(grad_att.astype(F32) * attended.astype(F32), axis=-1, keepdims=True)
        dprob = mm_nt(grad_att, value)
        dscore = (probs * (dprob - delta)).astype(BF)
        grad_q = (mm(dscore, key) * scale).astype(BF)
        grad_k = (mm_tn(dscore, query) * scale).astype(BF)
        grad_v = mm_tn(probs_b, grad_att).astype(BF)
        grads = jnp.concatenate([grad_q, grad_k, grad_v], axis=1)
        grad_act = cot_f.astype(F32) + mm_nt(grads, wqkv[...])
        scaled = grad_act * sigma * (1.0 + normed * (1.0 - sigma)) * g
        grad_conv = inverse * (
            scaled
            - convf * inverse * inverse * jnp.mean(scaled * convf, axis=-1, keepdims=True)
        )
        gc_full[1 : full + 1] = grad_conv.astype(BF).reshape(full, width, chans)
        gwin[f] = gc_full[pl.ds(row * h, h + 2)]
        if f < 2:
            back = remote(
                gwin.at[f], gwin.at[frames + f], gc_send.at[f], gc_recv.at[f], tm - 1, row
            )
            pl.when(has_prev)(back.start)
            backs.append(back)
        projected = mm(att_s[mine], wo[...])
        out = (act_s[mine].astype(F32) + projected).astype(BF)
        block_out[f] = out.reshape(h, width, chans)

    def back_step(a):
        lhs = jnp.concatenate(
            [
                gwin[2 - a : 2 - a + frames, 2 - b : 2 - b + h].reshape(own, chans)
                for b in range(TAPS)
            ],
            axis=1,
        )
        rhs = jnp.concatenate(
            [wbuf[a, b].reshape(TAPS * chans, chans) for b in range(TAPS)], axis=1
        )
        return mm_nt(lhs, rhs)

    sums[...] = back_step(2)
    for back in backs:
        pl.when(has_next)(back.wait_recv)
    sums[...] += back_step(1)
    sums[...] += back_step(0)
    result = shifted(part(0), -1) + part(1) + shifted(part(2), 1)
    video_grad[...] = result.astype(BF).reshape(frames, h, width, chans)

    for cond, copy, _ in halos:
        pl.when(cond)(copy.wait_send)
    for copy in cots + convs:
        copy.wait_send()
    for back in backs:
        pl.when(has_prev)(back.wait_send)


def local(n_tm, n_rows, video, conv_weight, norm_gain, w_query, w_key, w_value, w_out, cotangent):
    frames, h, width, chans = video.shape
    full = n_rows * h
    own = frames * h * width
    anywhere = pl.BlockSpec(memory_space=pl.ANY)
    vmem = pl.BlockSpec(memory_space=pltpu.VMEM)
    dma = pltpu.SemaphoreType.DMA
    shape = jax.ShapeDtypeStruct(video.shape, BF)
    return pl.pallas_call(
        functools.partial(block, n_tm, n_rows),
        out_shape=(shape, shape),
        in_specs=[anywhere, anywhere, vmem] + [anywhere] * 5,
        out_specs=(vmem, vmem),
        scratch_shapes=[
            pltpu.VMEM((frames + 2, h + 2, width, chans), BF),
            pltpu.VMEM(conv_weight.shape, BF),
            pltpu.VMEM((chans, 3 * chans), BF),
            pltpu.VMEM((chans, chans), BF),
            pltpu.VMEM((frames, full, width, chans), BF),
            pltpu.VMEM((frames, full, width, chans), BF),
            pltpu.VMEM((own, TAPS * chans), F32),
            pltpu.VMEM((full * width, chans), BF),
            pltpu.VMEM((full * width, chans), BF),
            pltpu.VMEM((full + 2, width, chans), BF),
            pltpu.VMEM((frames + 2, h + 2, width, chans), BF),
            dma((TAPS, TAPS)),
            dma((4,)),
            dma((2,)),
            dma((5,)),
            dma((5,)),
            dma((n_rows - 1,)),
            dma((n_rows - 1,)),
            dma((n_rows - 1,)),
            dma((n_rows - 1,)),
            dma((2,)),
            dma((2,)),
        ],
        compiler_params=pltpu.CompilerParams(
            collective_id=0, has_side_effects=True, vmem_limit_bytes=56 * 1024 * 1024
        ),
    )(
        video,
        conv_weight,
        norm_gain.reshape(1, chans),
        w_query,
        w_key,
        w_value,
        w_out,
        cotangent,
    )


def solution(mesh):
    n_tm, n_rows = mesh.shape["tm"], mesh.shape["rows"]
    split = P("tm", "rows", None, None)
    return jax.shard_map(
        functools.partial(local, n_tm, n_rows),
        mesh=mesh,
        in_specs=(split, P(), P(), P(), P(), P(), P(), split),
        out_specs=(split, split),
        check_vma=False,
    )
```

time: 114 us -> 38.4 us (0.34)
  Pallas kernels: 0 us -> 33 us
  blocking collectives: 32.7 us -> 0 us
  matrix products: 29.8 us -> 0 us
  starting transfers between devices: 22 us -> 0 us
  local copies, waits for them, and re-layouts: 16.7 us -> 4.49 us
  waiting for transfers between devices: 9.27 us -> 0 us
  other arithmetic: 1.95 us -> 0 us
    pallas_call x0 -> x1, Pallas kernels: none -> 33 us  [local(): pl.pallas_call(functools.partial(block, n_tm, n_rows), out_shape=(shape,...]
    all_gather x6 -> x0, blocking collectives: 32.7 us -> none  [the longest x1 7.38 us: local(): lax.all_gather(values, 'rows', axis=1, tiled=True)]
    ppermute x6 -> x0, starting transfers between devices: 22 us -> none  [the longest x4 16.8 us: from_behind(): return lax.ppermute(value, axis, pairs)]
    conv_general_dilated x2 -> x0, matrix products: 21.1 us -> none  [convolve(): lax.conv_general_dilated(padded[None], kernel, (1, 1, 1), pads, dimension...]
    ppermute x6 -> x0, waiting for transfers between devices: 9.27 us -> none  [the longest x4 6.19 us: from_behind(): return lax.ppermute(value, axis, pairs)]
    dot_general x14 -> x0, matrix products: 8.7 us -> none  [the longest x8 5.21 us: project(): jnp.dot(source.reshape(-1, source.shape[-1]), weight, preferred_element_t...]
    scatter-add x2 -> x0, local copies, waits for them, and re-layouts: 6.47 us -> none  [the longest x1 3.23 us: local(): inner = inner.at[:, 0].add(from_above)]
    convert_element_type x6 -> x0, local copies, waits for them, and re-layouts: 1.8 us -> none  [the longest x2 1.2 us: local(): convf = conv.astype(jnp.float32)]
  transfers between devices with their start and end apart: 6 -> 0, of which waited for: 3 -> 0; matrix products, arithmetic and copies ran while one was open for 7% -> 0% of each run, Pallas kernels for 0% -> 0%
where the time goes in v1:
time: 38.4 us; the launch traced here: 38.2 us
  Pallas kernels  33 us (86%)
  local copies, waits for them, and re-layouts  4.49 us (12%)
  between operations  0.64 us (2%)
    pallas_call x1, Pallas kernels, local(): pl.pallas_call(functools.partial(block, n_tm, n_rows), out_shape=(shape,...  33 us
    unnamed x2, local copies, waits for them, and re-layouts  3.25 us
    reshape x1, local copies, waits for them, and re-layouts, local(): norm_gain.reshape(1, chans)  1.25 us

profile of v1, /device:TPU:1, one launch (start us, length us, event | category | flops | bytes accessed | tf_op | source)
XLA Modules:
  0.0 38.2 jit_solution(9575378012798551706)
XLA Ops:
  0.6 1.2 %reshape.7.gain = f32[1,384]{1,0:T(1,128)} reshape(f32[384]{0:T(512)} %param.10) | data formatting | bytes 3072 | tf_op jit(solution)/shard_map/reshape | solution.py:347
  1.9 33.0 %shard_map.95 = (bf16[2,2,64,384]{3,2,1,0:T(8,128)(2,1)}, bf16[2,2,64,384]{3,2,1,0:T(8,128)(2,1)}) custom-call(bf16[2,2,64,384]{3,2,1,0:T(8,128)(2,1)} %video.1, bf16[3,3,3,384,384]{4,3,2,1,0:T(8,128)(2,1)} %weight.1, f32[1,384]{1,0:T(1,128)} %reshape.7.gain, bf16[384,384]{1,0:T(8,128)(2,1)} %w_query.1, bf16[384,384]{1,0:T(8,128)(2,1)} %w_key.1, ...), custom_call_target="tpu_custom_call" | custom-call | tf_op jit(solution)/shard_map/pallas_call | solution.py:312
  34.9 1.6 %copy.12 = bf16[2,2,64,384]{3,2,1,0:T(8,128)(2,1)} copy(bf16[2,2,64,384]{3,2,1,0:T(8,128)(2,1)} %get-tuple-element.4) | data formatting | bytes 393216
  36.5 1.6 %copy.13 = bf16[2,2,64,384]{3,2,1,0:T(8,128)(2,1)} copy(bf16[2,2,64,384]{3,2,1,0:T(8,128)(2,1)} %get-tuple-element.5) | data formatting | bytes 393216

commit v2 on v1

--- a/solution.py
+++ b/solution.py
@@ -47,6 +47,7 @@
     act_s,
     att_s,
     gc_full,
+    grad_s,
     gwin,
     w_sem,
     p_sem,
@@ -107,8 +108,6 @@
             barrier, inc=1, device_id=(tm, peer), device_id_type=pl.DeviceIdType.MESH
         )
     greet(has_prev, tm - 1, row)
-    greet(has_prev & has_up, tm - 1, row - 1)
-    greet(has_prev & has_down, tm - 1, row + 1)
     greet(has_next, tm + 1, row)
 
     line = jnp.zeros((frames, width, chans), BF)
@@ -137,7 +136,7 @@
     wait_for = (
         (n_rows - 1)
         + jnp.where(has_prev, 1, 0)
-        + jnp.where(has_next, 1 + jnp.where(has_up, 1, 0) + jnp.where(has_down, 1, 0), 0)
+        + jnp.where(has_next, 1, 0)
     )
     pl.semaphore_wait(barrier, wait_for)
 
@@ -157,9 +156,16 @@
     halos = [
         (has_up, remote(video.at[:, top], xin.at[now, pl.ds(h + 1, 1)], halo_send.at[0], halo_recv.at[0], tm, row - 1), has_down),
         (has_down, remote(video.at[:, low], xin.at[now, pl.ds(0, 1)], halo_send.at[1], halo_recv.at[1], tm, row + 1), has_up),
-        (has_next & has_up, remote(video.at[late, top], xin.at[before, pl.ds(h + 1, 1)], halo_send.at[2], halo_recv.at[2], tm + 1, row - 1), has_prev & has_down),
-        (has_next & has_down, remote(video.at[late, low], xin.at[before, pl.ds(0, 1)], halo_send.at[3], halo_recv.at[3], tm + 1, row + 1), has_prev & has_up),
-        (has_next, remote(video.at[late], xin.at[before, pl.ds(1, h)], halo_send.at[4], halo_recv.at[4], tm + 1, row), has_prev),
+        (has_next, remote(video.at[late], xin.at[before, pl.ds(1, h)], halo_send.at[2], halo_recv.at[2], tm + 1, row), has_prev),
+    ]
+    last = pl.ds(frames, 2)
+    edges = [
+        (cond, pl.ds(i, 1), halo_send.at[k], halo_recv.at[k])
+        for cond, i, k in ((has_up, 0, 3), (has_down, h + 1, 4))
+    ]
+    passed = [
+        (has_next & cond, remote(xin.at[last, i], xin.at[before, i], ss, rs, tm + 1, row), has_prev & cond)
+        for cond, i, ss, rs in edges
     ]
     for cond, copy, _ in halos:
         pl.when(cond)(copy.start)
@@ -186,16 +192,21 @@
     in_copy.wait()
     for _, copy, cond in halos[:2]:
         pl.when(cond)(copy.wait_recv)
+    for cond, copy, _ in passed:
+        pl.when(cond)(copy.start)
+    cots = [
+        remote(
+            cot.at[f], cot_full.at[f, own_rows], cot_send.at[f, k], cot_recv.at[f, k], tm, peer
+        )
+        for f in range(frames)
+        for k, peer in enumerate(peers)
+    ]
+    for copy in cots:
+        copy.start()
     for b in range(TAPS):
         w_copies[2, b].wait()
     sums[...] = conv_step(2)
-    cots = [
-        remote(cot, cot_full.at[:, own_rows], cot_send.at[k], cot_recv.at[k], tm, peer)
-        for k, peer in enumerate(peers)
-    ]
-    for copy in cots:
-        copy.start()
-    for _, copy, cond in halos[2:]:
+    for _, copy, cond in halos[2:] + passed:
         pl.when(cond)(copy.wait_recv)
     for a in (1, 0):
         for b in range(TAPS):
@@ -204,30 +215,36 @@
     conv = (shifted(part(0), 1) + part(1) + shifted(part(2), -1)).astype(BF)
     conv_full[:, own_rows] = conv.reshape(frames, h, width, chans)
     convs = [
-        remote(
-            conv_full.at[:, own_rows],
-            conv_full.at[:, own_rows],
-            conv_send.at[k],
-            conv_recv.at[k],
-            tm,
-            peer,
-        )
-        for k, peer in enumerate(peers)
-    ]
-    for copy in convs:
-        copy.start()
+        [
+            remote(
+                conv_full.at[f, own_rows],
+                conv_full.at[f, own_rows],
+                conv_send.at[f, k],
+                conv_recv.at[f, k],
+                tm,
+                peer,
+            )
+            for k, peer in enumerate(peers)
+        ]
+        for f in range(frames)
+    ]
+    for group in convs:
+        for copy in group:
+            copy.start()
     for c in p_copies:
         c.wait()
     cot_copy.wait()
     for copy in cots:
         copy.wait_recv()
-    for copy in convs:
-        copy.wait_recv()
-
-    g = gain[...]
+    for f in range(frames):
+        grad_s[f] = mm_nt(cot_full[f].reshape(pos, chans), wo[...]).astype(BF)
+
+    g = gain[...].reshape(1, chans)
     mine = pl.ds(pl.multiple_of(row * (h * width), h * width), h * width)
     backs = []
     for f in range(frames):
+        for copy in convs[f]:
+            copy.wait_recv()
         convf = conv_full[f].reshape(pos, chans).astype(F32)
         inverse = lax.rsqrt(jnp.mean(convf * convf, axis=-1, keepdims=True) + 1e-06)
         normed = convf * inverse * g
@@ -239,7 +256,7 @@
         key = qkv[:, chans : 2 * chans]
         value = qkv[:, 2 * chans :]
         cot_f = cot_full[f].reshape(pos, chans)
-        grad_att = mm_nt(cot_f, wo[...]).astype(BF)
+        grad_att = grad_s[f]
         scores = mm_nt(query, key) * scale
         peak = jnp.max(scores, axis=-1, keepdims=True)
         expo = jnp.exp(scores - peak)
@@ -286,19 +303,24 @@
         return mm_nt(lhs, rhs)
 
     sums[...] = back_step(2)
-    for back in backs:
-        pl.when(has_next)(back.wait_recv)
+    pl.when(has_next)(backs[0].wait_recv)
     sums[...] += back_step(1)
+    pl.when(has_next)(backs[1].wait_recv)
     sums[...] += back_step(0)
     result = shifted(part(0), -1) + part(1) + shifted(part(2), 1)
     video_grad[...] = result.astype(BF).reshape(frames, h, width, chans)
 
-    for cond, copy, _ in halos:
+    for cond, copy, _ in halos + passed:
         pl.when(cond)(copy.wait_send)
-    for copy in cots + convs:
+    for copy in sum(convs, cots):
         copy.wait_send()
     for back in backs:
         pl.when(has_prev)(back.wait_send)
+
+
+def settle(a, b, a_out, b_out):
+    a_out[...] = a[...]
+    b_out[...] = b[...]
 
 
 def local(n_tm, n_rows, video, conv_weight, norm_gain, w_query, w_key, w_value, w_out, cotangent):
@@ -309,7 +331,7 @@
     vmem = pl.BlockSpec(memory_space=pltpu.VMEM)
     dma = pltpu.SemaphoreType.DMA
     shape = jax.ShapeDtypeStruct(video.shape, BF)
-    return pl.pallas_call(
+    outs = pl.pallas_call(
         functools.partial(block, n_tm, n_rows),
         out_shape=(shape, shape),
         in_specs=[anywhere, anywhere, vmem] + [anywhere] * 5,
@@ -325,16 +347,17 @@
             pltpu.VMEM((full * width, chans), BF),
             pltpu.VMEM((full * width, chans), BF),
             pltpu.VMEM((full + 2, width, chans), BF),
+            pltpu.VMEM((frames, full * width, chans), BF),
             pltpu.VMEM((frames + 2, h + 2, width, chans), BF),
             dma((TAPS, TAPS)),
             dma((4,)),
             dma((2,)),
             dma((5,)),
             dma((5,)),
-            dma((n_rows - 1,)),
-            dma((n_rows - 1,)),
-            dma((n_rows - 1,)),
-            dma((n_rows - 1,)),
+            dma((frames, n_rows - 1)),
+            dma((frames, n_rows - 1)),
+            dma((frames, n_rows - 1)),
+            dma((frames, n_rows - 1)),
             dma((2,)),
             dma((2,)),
         ],
@@ -344,13 +367,19 @@
     )(
         video,
         conv_weight,
-        norm_gain.reshape(1, chans),
+        norm_gain,
         w_query,
         w_key,
         w_value,
         w_out,
         cotangent,
     )
+    return pl.pallas_call(
+        settle,
+        out_shape=(shape, shape),
+        in_specs=[vmem] * 2,
+        out_specs=(vmem, vmem),
+    )(*outs)
 
 
 def solution(mesh):

time: 38.4 us -> 30.5 us (0.79)
  local copies, waits for them, and re-layouts: 4.49 us -> 0 us
  Pallas kernels: 33 us -> 29.7 us
    pallas_call x1, Pallas kernels: 33 us -> 27.9 us  [local(): pl.pallas_call(functools.partial(block, n_tm, n_rows), out_shape=(shape,...]
    unnamed x2 -> x0, local copies, waits for them, and re-layouts: 3.25 us -> none
    pallas_call x0 -> x1, Pallas kernels: none -> 1.78 us  [local(): pl.pallas_call(settle, out_shape=(shape, shape), in_specs=[vmem] * 2, out...]
    reshape x1 -> x0, local copies, waits for them, and re-layouts: 1.25 us -> none  [local(): norm_gain.reshape(1, chans)]
where the time goes in v2:
time: 30.5 us; the launch traced here: 30.3 us
  Pallas kernels  29.7 us (97%)
  between operations  0.64 us (2%)
    pallas_call x1, Pallas kernels, local(): pl.pallas_call(functools.partial(block, n_tm, n_rows), out_shape=(shape,...  27.9 us
    pallas_call x1, Pallas kernels, local(): pl.pallas_call(settle, out_shape=(shape, shape), in_specs=[vmem] * 2, out...  1.78 us

profile of v2, /device:TPU:1, one launch (start us, length us, event | category | flops | bytes accessed | tf_op | source)
XLA Modules:
  0.0 30.3 jit_solution(11728762636813765126)
XLA Ops:
  0.6 27.9 %shard_map.95 = (bf16[2,2,64,384]{3,2,1,0:T(8,128)(2,1)}, bf16[2,2,64,384]{3,2,1,0:T(8,128)(2,1)}) custom-call(bf16[2,2,64,384]{3,2,1,0:T(8,128)(2,1)} %video.1, bf16[3,3,3,384,384]{4,3,2,1,0:T(8,128)(2,1)} %weight.1, f32[384]{0:T(512)} %gain.1, bf16[384,384]{1,0:T(8,128)(2,1)} %w_query.1, bf16[384,384]{1,0:T(8,128)(2,1)} %w_key.1, ...), custom_call_target="tpu_custom_call" | custom-call | tf_op jit(solution)/shard_map/pallas_call | solution.py:334
  28.5 1.8 %shard_map.96 = (bf16[2,2,64,384]{3,2,1,0:T(8,128)(2,1)}, bf16[2,2,64,384]{3,2,1,0:T(8,128)(2,1)}) custom-call(bf16[2,2,64,384]{3,2,1,0:T(8,128)(2,1)} %get-tuple-element.4.a, bf16[2,2,64,384]{3,2,1,0:T(8,128)(2,1)} %get-tuple-element.5.b), custom_call_target="tpu_custom_call" | custom-call | tf_op jit(solution)/shard_map/pallas_call | solution.py:377

commit v3 on v2

--- a/solution.py
+++ b/solution.py
@@ -170,14 +170,31 @@
     for cond, copy, _ in halos:
         pl.when(cond)(copy.start)
 
-    def conv_step(a):
+    cots = [
+        remote(
+            cot.at[f], cot_full.at[f, own_rows], cot_send.at[f, k], cot_recv.at[f, k], tm, peer
+        )
+        for f in range(frames)
+        for k, peer in enumerate(peers)
+    ]
+    for copy in cots[: len(peers)]:
+        copy.start()
+
+    def conv_step(taps):
         lhs = jnp.concatenate(
-            [xin[a : a + frames, b : b + h].reshape(own, chans) for b in range(TAPS)], axis=1
+            [xin[a : a + frames, pl.ds(b, h)].reshape(own, chans) for a, b in taps], axis=1
         )
         rhs = jnp.concatenate(
-            [wbuf[a, :, c].reshape(TAPS * chans, chans) for c in range(TAPS)], axis=1
+            [
+                jnp.concatenate([wbuf[a, b, c] for a, b in taps], axis=0)
+                for c in range(TAPS)
+            ],
+            axis=1,
         )
         return mm(lhs, rhs)
+
+    near = jnp.where(first_row, 0, 2)
+    far = 2 - near
 
     column = lax.rem(lax.broadcasted_iota(jnp.int32, (own, 1), 0), width)
 
@@ -190,28 +207,25 @@
         return sums[:, c * chans : (c + 1) * chans]
 
     in_copy.wait()
-    for _, copy, cond in halos[:2]:
-        pl.when(cond)(copy.wait_recv)
+    for b in range(TAPS):
+        w_copies[2, b].wait()
+    pl.when(has_down & has_up)(halos[0][1].wait_recv)
+    sums[...] = conv_step([(2, 1), (2, near)])
+    pl.when(has_down & first_row)(halos[0][1].wait_recv)
+    pl.when(has_up)(halos[1][1].wait_recv)
     for cond, copy, _ in passed:
         pl.when(cond)(copy.start)
-    cots = [
-        remote(
-            cot.at[f], cot_full.at[f, own_rows], cot_send.at[f, k], cot_recv.at[f, k], tm, peer
-        )
-        for f in range(frames)
-        for k, peer in enumerate(peers)
-    ]
-    for copy in cots:
+    for copy in cots[len(peers) :]:
         copy.start()
-    for b in range(TAPS):
-        w_copies[2, b].wait()
-    sums[...] = conv_step(2)
-    for _, copy, cond in halos[2:] + passed:
-        pl.when(cond)(copy.wait_recv)
     for a in (1, 0):
         for b in range(TAPS):
             w_copies[a, b].wait()
-        sums[...] += conv_step(a)
+    pl.when(has_prev)(halos[2][1].wait_recv)
+    pl.when(has_prev & has_down & has_up)(passed[1][1].wait_recv)
+    sums[...] += conv_step([(1, 1), (1, near), (0, 1), (0, near)])
+    pl.when(has_prev & has_down & first_row)(passed[1][1].wait_recv)
+    pl.when(has_prev & has_up)(passed[0][1].wait_recv)
+    sums[...] += conv_step([(2, far), (1, far), (0, far)])
     conv = (shifted(part(0), 1) + part(1) + shifted(part(2), -1)).astype(BF)
     conv_full[:, own_rows] = conv.reshape(frames, h, width, chans)
     convs = [
@@ -234,15 +248,13 @@
     for c in p_copies:
         c.wait()
     cot_copy.wait()
-    for copy in cots:
-        copy.wait_recv()
-    for f in range(frames):
-        grad_s[f] = mm_nt(cot_full[f].reshape(pos, chans), wo[...]).astype(BF)
-
     g = gain[...].reshape(1, chans)
     mine = pl.ds(pl.multiple_of(row * (h * width), h * width), h * width)
     backs = []
     for f in range(frames):
+        for copy in cots[f * len(peers) : (f + 1) * len(peers)]:
+            copy.wait_recv()
+        grad_s[f] = mm_nt(cot_full[f].reshape(pos, chans), wo[...]).astype(BF)
         for copy in convs[f]:
             copy.wait_recv()
         convf = conv_full[f].reshape(pos, chans).astype(F32)

time: 30.5 us -> 29.7 us (0.974)
  Pallas kernels: 29.7 us -> 28.8 us
    pallas_call x1, Pallas kernels: 27.9 us -> 27.1 us  [local(): pl.pallas_call(functools.partial(block, n_tm, n_rows), out_shape=(shape,...]
where the time goes in v3:
time: 29.7 us; the launch traced here: 29.5 us
  Pallas kernels  28.8 us (97%)
  between operations  0.64 us (2%)
    pallas_call x1, Pallas kernels, local(): pl.pallas_call(functools.partial(block, n_tm, n_rows), out_shape=(shape,...  27.1 us
    pallas_call x1, Pallas kernels, local(): pl.pallas_call(settle, out_shape=(shape, shape), in_specs=[vmem] * 2, out...  1.78 us

profile of v3, /device:TPU:1, one launch (start us, length us, event | category | flops | bytes accessed | tf_op | source)
XLA Modules:
  0.0 29.5 jit_solution(671621896119181433)
XLA Ops:
  0.6 27.1 %shard_map.95 = (bf16[2,2,64,384]{3,2,1,0:T(8,128)(2,1)}, bf16[2,2,64,384]{3,2,1,0:T(8,128)(2,1)}) custom-call(bf16[2,2,64,384]{3,2,1,0:T(8,128)(2,1)} %video.1, bf16[3,3,3,384,384]{4,3,2,1,0:T(8,128)(2,1)} %weight.1, f32[384]{0:T(512)} %gain.1, bf16[384,384]{1,0:T(8,128)(2,1)} %w_query.1, bf16[384,384]{1,0:T(8,128)(2,1)} %w_key.1, ...), custom_call_target="tpu_custom_call" | custom-call | tf_op jit(solution)/shard_map/pallas_call | solution.py:346
  27.7 1.8 %shard_map.96 = (bf16[2,2,64,384]{3,2,1,0:T(8,128)(2,1)}, bf16[2,2,64,384]{3,2,1,0:T(8,128)(2,1)}) custom-call(bf16[2,2,64,384]{3,2,1,0:T(8,128)(2,1)} %get-tuple-element.4.a, bf16[2,2,64,384]{3,2,1,0:T(8,128)(2,1)} %get-tuple-element.5.b), custom_call_target="tpu_custom_call" | custom-call | tf_op jit(solution)/shard_map/pallas_call | solution.py:389
